TPU v7x, 512 devices: a whole 4x4x16 slice. The times are simulated.
512 devices in a mesh: expert: 128 (over z, y, core), token: 4 (over x).
Axes of the slice: x: 4, y: 4, z: 16, core: 2. Of those that a mesh axis runs over, the one named last changes fastest.
Arguments:
- tokens: bfloat16 [8192, 2048], P(('expert', 'token')), may hold values from -6 to 6
- routes: int32 [8192, 8], P(('expert', 'token')), may hold values from 0 to 127, all different within a row; in each aligned block of 16 rows (0 to 15, 16 to 31, ...) at most 2 rows name the same one
- assign: int32 [128], replicated, may hold values from 0 to 31, as said below
- gate_weight: bfloat16 [128, 2048, 1536], P('expert', None, 'token'), may hold values from -0.125 to 0.125
- up_weight: bfloat16 [128, 2048, 1536], P('expert', None, 'token'), may hold values from -0.125 to 0.125
- sketch: bfloat16 [128, 1536, 512], P('expert', 'token'), may hold values from -6 to 6
Outputs:
- hidden: bfloat16 [128, 1024, 1536], P('expert', None, 'token')
Inputs may be any that keep to these rules, and one draw needn't show every extreme that they name: `routes`: within each aligned block of 16 tokens each token names 8 different experts, and no expert is named by more than 2 entries of the block. `assign`: every one of the 32 clusters has at least two experts.
All inputs are finite; a program needn't handle non-finite values.
Results may differ from a plain program's by a relative error of at most 0.029.
Values may be sent and summed in bfloat16 or wider, within the bound.
A program may use at most 64 MiB of HBM per device.

v0:
```python
import jax
import jax.numpy as jnp
from jax import lax
from jax.sharding import PartitionSpec as P


def place_tokens(tok_rows, tok_ids, expert_count, capacity):
    flat_ids = tok_ids.reshape(-1)
    expert_hits = (flat_ids[:, None] == jnp.arange(expert_count, dtype=jnp.int32)[None, :]).astype(
        jnp.int32
    )
    earlier = jnp.cumsum(expert_hits, axis=0) - expert_hits
    slot_index = jnp.sum(earlier * expert_hits, axis=1)
    target = flat_ids * capacity + slot_index
    select = (
        jnp.arange(expert_count * capacity, dtype=jnp.int32)[:, None] == target[None, :]
    ).astype(jnp.float32)
    select = (
        select.reshape(expert_count * capacity, tok_rows.shape[0], tok_ids.shape[1])
        .sum(axis=2)
        .astype(jnp.bfloat16)
    )
    filled = jnp.dot(select, tok_rows, preferred_element_type=jnp.float32).astype(jnp.bfloat16)
    return filled.reshape(expert_count, capacity, tok_rows.shape[1])


def new_basis(partial_term, member, assign, token_count, expert_count):
    rank_cols = partial_term.shape[1]
    row_block = partial_term.shape[0] // (token_count * expert_count)
    pieces = partial_term.reshape(token_count, expert_count * row_block, rank_cols)
    arrived = lax.all_to_all(pieces, "expert", split_axis=1, concat_axis=1, tiled=True)
    arrived = arrived.reshape(token_count, expert_count, row_block, rank_cols)
    by_cluster = jnp.einsum("ci,tirk->ctrk", member, arrived, preferred_element_type=jnp.float32)
    own_rows = lax.psum_scatter(
        by_cluster.astype(jnp.bfloat16), "token", scatter_dimension=1, tiled=True
    ).astype(jnp.float32)
    outgoing = jnp.take(own_rows[:, 0], assign, axis=0).astype(jnp.bfloat16)
    returned = lax.all_to_all(outgoing, "expert", split_axis=0, concat_axis=0, tiled=True)
    cluster_rows = returned.reshape(expert_count * row_block, rank_cols)
    local_gram = lax.dot_general(
        cluster_rows, cluster_rows, (((0,), (0,)), ((), ())), preferred_element_type=jnp.float32
    )
    column_gram = lax.psum(local_gram.astype(jnp.bfloat16), "token").astype(jnp.float32)
    lower_factor = jnp.linalg.cholesky(column_gram)
    solved = jax.scipy.linalg.solve_triangular(
        lower_factor, cluster_rows.astype(jnp.float32).T, lower=True
    )
    basis_part = solved.T.astype(jnp.bfloat16)
    return lax.all_gather(basis_part, "token", axis=0, tiled=True)


def per_device(tokens, routes, assign, gate_weight, up_weight, sketch):
    expert_count = lax.axis_size("expert")
    token_count = lax.axis_size("token")
    cluster_count = expert_count // 4
    gate_local = gate_weight[0]
    up_local = up_weight[0]
    member = (assign[None, :] == jnp.arange(cluster_count, dtype=jnp.int32)[:, None]).astype(
        jnp.bfloat16
    )
    partial_term = jnp.dot(up_local, sketch[0], preferred_element_type=jnp.float32).astype(
        jnp.bfloat16
    )
    basis = new_basis(partial_term, member, assign, token_count, expert_count)
    projected = lax.dot_general(
        up_local, basis, (((0,), (0,)), ((), ())), preferred_element_type=jnp.float32
    ).astype(jnp.bfloat16)
    partial_term = jnp.dot(up_local, projected, preferred_element_type=jnp.float32).astype(
        jnp.bfloat16
    )
    basis = new_basis(partial_term, member, assign, token_count, expert_count)
    shard_rows = tokens.shape[0]
    capacity = max(2, 2 * shard_rows * routes.shape[1] // expert_count)
    outgoing = place_tokens(tokens, routes, expert_count, capacity)
    arrived = lax.all_to_all(outgoing, "expert", split_axis=0, concat_axis=0, tiled=True)
    slots_in = lax.all_gather(arrived, "token", axis=0, tiled=True)
    slots_in = slots_in.reshape(-1, tokens.shape[1])
    gate_value = jnp.dot(slots_in, gate_local, preferred_element_type=jnp.float32)
    on_basis = jnp.dot(slots_in, basis, preferred_element_type=jnp.float32).astype(jnp.bfloat16)
    coefficient = lax.dot_general(
        basis, up_local, (((0,), (0,)), ((), ())), preferred_element_type=jnp.float32
    ).astype(jnp.bfloat16)
    merged = jnp.dot(on_basis, coefficient, preferred_element_type=jnp.float32)
    hidden = (jax.nn.silu(gate_value) * merged).astype(jnp.bfloat16)
    return hidden[None]


def solution(mesh):
    return jax.shard_map(
        per_device,
        mesh=mesh,
        in_specs=(
            P(("expert", "token"), None),
            P(("expert", "token"), None),
            P(),
            P("expert", None, "token"),
            P("expert", None, "token"),
            P("expert", "token", None),
        ),
        out_specs=P("expert", None, "token"),
        check_vma=False,
    )
```

profile of v0, /device:TPU:1, one launch (start us, length us, event | category | flops | bytes accessed | tf_op | source)
XLA Modules:
  0.0 931.0 jit_solution(862876491536003445)
XLA Ops:
  7.9 2.2 convolution_convert_fusion.1
  11.8 117.2 %all_to_all.25 = bf16[4,512,512]{2,0,1:T(4,128)(2,1)S(1)} all-to-all(bf16[4,512,512]{2,0,1:T(4,128)(2,1)S(1)} %copy.53), channel_id=1, replica_groups=mesh['expert'=128,'token'=4] {'expert'}, dimensions={1} | all-to-all | bytes 4194304 | tf_op jit(solution)/shard_map/all_to_all | solution.py:31
  129.1 3.2 fusion.16
  132.4 22.3 %reduce-scatter.3.cloned.1.call-done = bf16[32,1,4,512]{3,0,2,1:T(8,128)(2,1)} async-done(((bf16[32,4,4,512]{3,0,2,1:T(8,128)(2,1)}), bf16[32,1,4,512]{3,0,2,1:T(8,128)(2,1)}) %reduce-scatter.3.cloned.1.call-update) | async-done | bytes 131088 | tf_op jit(solution)/shard_map/reduce_scatter | solution.py:34
  157.0 48.9 %all_to_all.26 = bf16[128,4,512]{2,1,0:T(4,128)(2,1)S(1)} all-to-all(bf16[128,4,512]{2,1,0:T(4,128)(2,1)S(1)} %select_convert_fusion.1), channel_id=1, replica_groups=mesh['expert'=128,'token'=4] {'expert'}, dimensions={0} | all-to-all | bytes 1048576 | tf_op jit(solution)/shard_map/all_to_all | solution.py:38
  208.9 47.0 %all-reduce.4.cloned.1.call-done = bf16[512,512]{0,1:T(8,128)(2,1)} async-done(((bf16[512,512]{0,1:T(8,128)(2,1)}), bf16[512,512]{0,1:T(8,128)(2,1)}) %all-reduce.4.cloned.1.call-update) | async-done | bytes 524304 | tf_op jit(solution)/shard_map/psum | solution.py:43
  259.4 11.7 %cholesky.286 = f32[128,128]{1,0:T(8,128)S(1)} custom-call(f32[128,128]{1,0:T(8,128)S(1)} %cholesky.426), custom_call_target="Cholesky" | custom-call | tf_op jit(solution)/shard_map/jit(cholesky)/cholesky | solution.py:44
  271.2 9.8 %custom-call.27 = f32[1,128,128]{1,2,0:T(8,128)S(1)} custom-call(f32[1,128,128]{2,1,0:T(8,128)S(1)} %get-tuple-element.63), custom_call_target="InvertDiagBlocksLowerTriangular" | custom-call | tf_op jit(solution)/shard_map/jit(cholesky)/cholesky | solution.py:44
  283.6 11.7 %cholesky.305 = f32[128,128]{1,0:T(8,128)S(1)} custom-call(f32[128,128]{1,0:T(8,128)S(1)} %cholesky.430), custom_call_target="Cholesky" | custom-call | tf_op jit(solution)/shard_map/jit(cholesky)/cholesky | solution.py:44
  295.4 10.0 %custom-call.28 = f32[1,128,128]{1,2,0:T(8,128)S(1)} custom-call(f32[1,128,128]{2,1,0:T(8,128)S(1)} %get-tuple-element.60), custom_call_target="InvertDiagBlocksLowerTriangular" | custom-call | tf_op jit(solution)/shard_map/jit(cholesky)/cholesky | solution.py:44
  307.0 11.7 %cholesky.326 = f32[128,128]{1,0:T(8,128)S(1)} custom-call(f32[128,128]{1,0:T(8,128)S(1)} %cholesky.435), custom_call_target="Cholesky" | custom-call | tf_op jit(solution)/shard_map/jit(cholesky)/cholesky | solution.py:44
  319.4 9.8 %custom-call.29 = f32[1,128,128]{1,2,0:T(8,128)S(1)} custom-call(f32[1,128,128]{2,1,0:T(8,128)S(1)} %get-tuple-element.57), custom_call_target="InvertDiagBlocksLowerTriangular" | custom-call | tf_op jit(solution)/shard_map/jit(cholesky)/cholesky | solution.py:44
  330.6 11.7 %cholesky.343 = f32[128,128]{1,0:T(8,128)S(1)} custom-call(f32[128,128]{1,0:T(8,128)S(1)} %convolution_subtract_fusion.11), custom_call_target="Cholesky" | custom-call | tf_op jit(solution)/shard_map/jit(cholesky)/cholesky | solution.py:44
  347.8 11.5 %while.4 = (s32[]{:T(128)}, f32[512,512]{1,0:T(8,128)}, s32[4,2]{0,1:T(2,128)S(1)}, f32[4,128,128]{2,1,0:T(8,128)S(1)}, s32[]{:T(128)}) while((s32[]{:T(128)}, f32[512,512]{1,0:T(8,128)}, s32[4,2]{0,1:T(2,128)S(1)}, f32[4,128,128]{2,1,0:T(8,128)S(1)}, s32[]{:T(128)}) %tuple.52), condition=%wide.while_cond, body=%wide.while_body.sunk | while | flops 2 | bytes 131189 | solution.py:45
  348.5 2.3 bitcast_dynamic-update-slice_fusion.4
  351.4 2.3 bitcast_dynamic-update-slice_fusion.4
  354.3 2.3 bitcast_dynamic-update-slice_fusion.4
  357.2 2.2 bitcast_dynamic-update-slice_fusion.4
  359.4 39.3 %custom-call.30 = f32[4,128,128]{1,2,0:T(8,128)S(1)} custom-call(f32[4,128,128]{2,1,0:T(8,128)S(1)} %get-tuple-element.22), custom_call_target="InvertDiagBlocksLowerTriangular" | custom-call | tf_op jit(solution)/shard_map/jit(_solve_triangular)/triangular_solve | solution.py:45
  406.5 41.5 %all-gather.6.cloned.1.call-done = bf16[2048,512]{0,1:T(8,128)(2,1)} async-done(((bf16[512,512]{0,1:T(8,128)(2,1)}), bf16[2048,512]{0,1:T(8,128)(2,1)}) %all-gather.6.cloned.1.call-update) | async-done | bytes 2097168 | tf_op jit(solution)/shard_map/all_gather | solution.py:49
  448.0 5.3 fusion
  453.3 4.5 reshape.84
  457.8 6.5 copy.61
  464.3 113.7 %all_to_all.27 = bf16[4,512,512]{2,0,1:T(4,128)(2,1)S(1)} all-to-all(bf16[4,512,512]{2,0,1:T(4,128)(2,1)} %copy.61), channel_id=1, replica_groups=mesh['expert'=128,'token'=4] {'expert'}, dimensions={1} | all-to-all | bytes 4194304 | tf_op jit(solution)/shard_map/all_to_all | solution.py:31
  578.0 3.2 fusion.19
  581.2 21.1 %reduce-scatter.5.cloned.1.call-done = bf16[32,1,4,512]{3,0,2,1:T(8,128)(2,1)} async-done(((bf16[32,4,4,512]{3,0,2,1:T(8,128)(2,1)}), bf16[32,1,4,512]{3,0,2,1:T(8,128)(2,1)}) %reduce-scatter.5.cloned.1.call-update) | async-done | bytes 131088 | tf_op jit(solution)/shard_map/reduce_scatter | solution.py:34
  605.5 18.3 %all-to-all-start.4 = ((bf16[128,4,512]{2,1,0:T(4,128)(2,1)}), bf16[128,4,512]{2,1,0:T(4,128)(2,1)S(1)}, u32[]{:S(2)}, u32[]{:S(2)}) async-start(bf16[128,4,512]{2,1,0:T(4,128)(2,1)} %select_convert_fusion), calls=%async_computation.6 | async-start | bytes 1048576 | tf_op jit(solution)/shard_map/all_to_all | solution.py:38
  626.6 28.0 %all-to-all-done.4 = bf16[128,4,512]{2,1,0:T(4,128)(2,1)S(1)} async-done(((bf16[128,4,512]{2,1,0:T(4,128)(2,1)}), bf16[128,4,512]{2,1,0:T(4,128)(2,1)S(1)}, u32[]{:S(2)}, u32[]{:S(2)}) %all-to-all-start.4) | async-done | bytes 524320 | tf_op jit(solution)/shard_map/all_to_all | solution.py:38
  654.6 9.1 all-to-all-start
  665.1 50.4 %all-to-all-done = bf16[128,2,2048]{2,1,0:T(2,128)(2,1)S(1)} async-done(((bf16[128,2,2048]{2,1,0:T(2,128)(2,1)}), bf16[128,2,2048]{2,1,0:T(2,128)(2,1)S(1)}, u32[]{:S(2)}, u32[]{:S(2)}) %all-to-all-start) | async-done | bytes 1048608 | tf_op jit(solution)/shard_map/all_to_all | solution.py:75
  718.2 4.0 all-reduce.6.cloned.1.call-done
  725.7 11.7 %cholesky.358 = f32[128,128]{1,0:T(8,128)S(1)} custom-call(f32[128,128]{1,0:T(8,128)S(1)} %cholesky.439), custom_call_target="Cholesky" | custom-call | tf_op jit(solution)/shard_map/jit(cholesky)/cholesky | solution.py:44
  737.4 9.8 %custom-call.31 = f32[1,128,128]{1,2,0:T(8,128)S(1)} custom-call(f32[1,128,128]{2,1,0:T(8,128)S(1)} %get-tuple-element.53), custom_call_target="InvertDiagBlocksLowerTriangular" | custom-call | tf_op jit(solution)/shard_map/jit(cholesky)/cholesky | solution.py:44
  749.9 11.7 %cholesky.377 = f32[128,128]{1,0:T(8,128)S(1)} custom-call(f32[128,128]{1,0:T(8,128)S(1)} %cholesky.443), custom_call_target="Cholesky" | custom-call | tf_op jit(solution)/shard_map/jit(cholesky)/cholesky | solution.py:44
  761.7 10.2 %custom-call.32 = f32[1,128,128]{1,2,0:T(8,128)S(1)} custom-call(f32[1,128,128]{2,1,0:T(8,128)S(1)} %get-tuple-element.50), custom_call_target="InvertDiagBlocksLowerTriangular" | custom-call | tf_op jit(solution)/shard_map/jit(cholesky)/cholesky | solution.py:44
  773.4 11.7 %cholesky.398 = f32[128,128]{1,0:T(8,128)S(1)} custom-call(f32[128,128]{1,0:T(8,128)S(1)} %cholesky.448), custom_call_target="Cholesky" | custom-call | tf_op jit(solution)/shard_map/jit(cholesky)/cholesky | solution.py:44
  785.2 9.8 %custom-call.33 = f32[1,128,128]{1,2,0:T(8,128)S(1)} custom-call(f32[1,128,128]{2,1,0:T(8,128)S(1)} %get-tuple-element.47), custom_call_target="InvertDiagBlocksLowerTriangular" | custom-call | tf_op jit(solution)/shard_map/jit(cholesky)/cholesky | solution.py:44
  796.4 11.7 %cholesky.415 = f32[128,128]{1,0:T(8,128)S(1)} custom-call(f32[128,128]{1,0:T(8,128)S(1)} %convolution_subtract_fusion.10), custom_call_target="Cholesky" | custom-call | tf_op jit(solution)/shard_map/jit(cholesky)/cholesky | solution.py:44
  814.6 11.3 %while.5 = (s32[]{:T(128)}, f32[512,512]{1,0:T(8,128)}, s32[4,2]{0,1:T(2,128)S(1)}, f32[4,128,128]{2,1,0:T(8,128)S(1)}, s32[]{:T(128)}) while((s32[]{:T(128)}, f32[512,512]{1,0:T(8,128)}, s32[4,2]{0,1:T(2,128)S(1)}, f32[4,128,128]{2,1,0:T(8,128)S(1)}, s32[]{:T(128)}) %tuple.72), condition=%wide.while_cond.clone, body=%wide.while_body.clone.sunk | while | flops 2 | bytes 131189 | solution.py:45
  815.2 2.2 bitcast_dynamic-update-slice_fusion.5
  818.0 2.2 bitcast_dynamic-update-slice_fusion.5
  820.9 2.2 bitcast_dynamic-update-slice_fusion.5
  825.9 39.3 %custom-call.34 = f32[4,128,128]{1,2,0:T(8,128)S(1)} custom-call(f32[4,128,128]{2,1,0:T(8,128)S(1)} %get-tuple-element.23), custom_call_target="InvertDiagBlocksLowerTriangular" | custom-call | tf_op jit(solution)/shard_map/jit(_solve_triangular)/triangular_solve | solution.py:45
  873.1 7.3 reshape.81
  880.4 5.7 fusion.11
  886.0 28.3 %all-gather.8.cloned.1.call-done = bf16[2048,512]{0,1:T(8,128)(2,1)} async-done(((bf16[512,512]{0,1:T(8,128)(2,1)}), bf16[2048,512]{0,1:T(8,128)(2,1)}) %all-gather.8.cloned.1.call-update) | async-done | bytes 2097168 | tf_op jit(solution)/shard_map/all_gather | solution.py:49
  914.3 2.8 fusion.25
  917.2 6.7 fusion.13
  (141 shorter events, 66.9 us)
Async XLA Ops:
  6.5 1.4 copy-start
  6.5 148.1 %reduce-scatter.3.cloned.1.call-start = ((), (), s32[]{:S(2)}) async-start(), calls=%async_computation.8 | async-start | bytes 655360 | tf_op jit(solution)/shard_map/reduce_scatter | solution.py:34
  11.8 117.2 %copy-start.8 = (s32[128]{0:T(128)S(1)}, s32[128]{0:T(128)}, u32[]{:S(2)}) copy-start(s32[128]{0:T(128)} %param.13) | copy-start | bytes 1540
  132.3 123.6 %all-reduce.4.cloned.1.call-start = ((), (), s32[]{:S(2)}) async-start(), calls=%async_computation.9 | async-start | bytes 1048576 | tf_op jit(solution)/shard_map/psum | solution.py:43
  207.3 240.8 %all-gather.6.cloned.1.call-start = ((), (), s32[]{:S(2)}) async-start(), calls=%async_computation.10 | async-start | bytes 2621440 | tf_op jit(solution)/shard_map/all_gather | solution.py:49
  258.4 1.0 copy-start.4
  347.8 54.0 %copy-start.2 = (f32[512,512]{0,1:T(8,128)S(1)}, f32[512,512]{0,1:T(8,128)}, u32[]{:S(2)}) copy-start(f32[512,512]{0,1:T(8,128)} %copy.60) | copy-start | bytes 3145732
  406.5 195.8 %reduce-scatter.5.cloned.1.call-start = ((), (), s32[]{:S(2)}) async-start(), calls=%async_computation.11 | async-start | bytes 655360 | tf_op jit(solution)/shard_map/reduce_scatter | solution.py:34
  581.2 42.6 %copy-start.7 = (s32[16,8]{0,1:T(8,128)S(1)}, s32[16,8]{0,1:T(8,128)}, u32[]{:S(2)}) copy-start(s32[16,8]{0,1:T(8,128)} %param.12) | copy-start | bytes 1540
  581.2 43.4 %copy-start.6 = (bf16[16,2048]{1,0:T(8,128)(2,1)S(1)}, bf16[16,2048]{1,0:T(8,128)(2,1)}, u32[]{:S(2)}) copy-start(bf16[16,2048]{1,0:T(8,128)(2,1)} %param.11) | copy-start | bytes 196612
  605.5 49.1 %all-to-all-start.4 = ((bf16[128,4,512]{2,1,0:T(4,128)(2,1)}), bf16[128,4,512]{2,1,0:T(4,128)(2,1)S(1)}, u32[]{:S(2)}, u32[]{:S(2)}) async-start(bf16[128,4,512]{2,1,0:T(4,128)(2,1)} %select_convert_fusion), calls=%async_computation.6 | async-start | bytes 1048576 | tf_op jit(solution)/shard_map/all_to_all | solution.py:38
  654.6 61.0 %all-to-all-start = ((bf16[128,2,2048]{2,1,0:T(2,128)(2,1)}), bf16[128,2,2048]{2,1,0:T(2,128)(2,1)S(1)}, u32[]{:S(2)}, u32[]{:S(2)}) async-start(bf16[128,2,2048]{2,1,0:T(2,128)(2,1)} %reshape.80), calls=%async_computation | async-start | bytes 2097152 | tf_op jit(solution)/shard_map/all_to_all | solution.py:75
  663.7 58.5 %all-reduce.6.cloned.1.call-start = ((), (), s32[]{:S(2)}) async-start(), calls=%async_computation.12 | async-start | bytes 1048576 | tf_op jit(solution)/shard_map/psum | solution.py:43
  665.1 208.0 %all-gather.4.cloned.1.call-start = ((), (), s32[]{:S(2)}) async-start(), calls=%async_computation.7 | async-start | bytes 5242880 | tf_op jit(solution)/shard_map/all_gather | solution.py:76
  715.5 1.0 copy-start.1
  716.5 197.8 %all-gather.8.cloned.1.call-start = ((), (), s32[]{:S(2)}) async-start(), calls=%async_computation.13 | async-start | bytes 2621440 | tf_op jit(solution)/shard_map/all_gather | solution.py:49
  724.7 1.0 copy-start.5
  814.5 53.8 %copy-start.3 = (f32[512,512]{0,1:T(8,128)S(1)}, f32[512,512]{0,1:T(8,128)}, u32[]{:S(2)}) copy-start(f32[512,512]{0,1:T(8,128)} %copy.68) | copy-start | bytes 3145732
  873.0 7.4 copy-start.9
  886.0 31.1 %copy-start.10 = (f32[1024,384]{1,0:T(8,128)S(1)}, f32[1024,384]{1,0:T(8,128)}, u32[]{:S(2)}) copy-start(f32[1024,384]{1,0:T(8,128)} %fusion.11) | copy-start | bytes 4718596
Sparse Core Ops, SparseCore 0:
  132.4 22.2 reduce-scatter.2
  207.4 48.4 all-reduce.3
  406.6 41.3 all-gather.5
  581.3 20.9 reduce-scatter.4
  666.6 55.6 all-reduce.5
  724.2 58.8 all-gather.3
  873.1 41.1 all-gather.7
where the time goes:
time: 940 us; the launch traced here: 931 us
  blocking collectives  280 us (30%)
  other arithmetic  246 us (26%)
  waiting for transfers between devices  243 us (26%)
  local copies, waits for them, and re-layouts  58.5 us (6%)
  matrix products  56.9 us (6%)
  starting transfers between devices  28 us (3%)
  between operations  19.3 us (2%)
    all_to_all x2, blocking collectives, new_basis(): lax.all_to_all(pieces, 'expert', split_axis=1, concat_axis=1, tiled=True)  231 us
    another operation x29, other arithmetic, new_basis(): lower_factor = jnp.linalg.cholesky(column_gram)  159 us
    another operation x5, other arithmetic, new_basis(): jax.scipy.linalg.solve_triangular(lower_factor, cluster_rows.astype(jnp.f...  80.9 us
    all_gather x2, waiting for transfers between devices, new_basis(): return lax.all_gather(basis_part, 'token', axis=0, tiled=True)  69.8 us
    psum x2, waiting for transfers between devices, new_basis(): lax.psum(local_gram.astype(jnp.bfloat16), 'token').astype(jnp.float32)  51 us
    all_to_all x1, waiting for transfers between devices, per_device(): lax.all_to_all(outgoing, 'expert', split_axis=0, concat_axis=0, tiled=True)  50.4 us
    all_to_all x1, blocking collectives, new_basis(): lax.all_to_all(outgoing, 'expert', split_axis=0, concat_axis=0, tiled=True)  48.9 us
    reduce_scatter x2, waiting for transfers between devices, new_basis(): lax.psum_scatter(by_cluster.astype(jnp.bfloat16), 'token', scatter_dimens...  43.4 us
  transfers between devices with their start and end apart: 9, of which 8 were waited for; matrix products, arithmetic and copies ran while one was open for 18% of the time, Pallas kernels for 0%

commit v1 on v0

--- a/solution.py
+++ b/solution.py
@@ -2,6 +2,27 @@
 import jax.numpy as jnp
 from jax import lax
 from jax.sharding import PartitionSpec as P
+
+
+def gather_around(x, axis, dim):
+    size, index, extent = (lax.axis_size(axis), lax.axis_index(axis), x.shape[dim])
+    forward = [(i, (i + 1) % size) for i in range(size)]
+    backward = [(i, (i - 1) % size) for i in range(size)]
+    filled = jnp.zeros((*x.shape[:dim], size * extent, *x.shape[dim + 1 :]), x.dtype)
+    filled = lax.dynamic_update_slice_in_dim(filled, x, index * extent, axis=dim)
+    from_left = from_right = x
+    half = size // 2
+    for lap in range(1, half + 1):
+        from_left = lax.ppermute(from_left, axis, forward)
+        filled = lax.dynamic_update_slice_in_dim(
+            filled, from_left, (index - lap) % size * extent, axis=dim
+        )
+        if lap < size - half:
+            from_right = lax.ppermute(from_right, axis, backward)
+            filled = lax.dynamic_update_slice_in_dim(
+                filled, from_right, (index + lap) % size * extent, axis=dim
+            )
+    return filled
 
 
 def place_tokens(tok_rows, tok_ids, expert_count, capacity):
@@ -46,7 +67,7 @@
         lower_factor, cluster_rows.astype(jnp.float32).T, lower=True
     )
     basis_part = solved.T.astype(jnp.bfloat16)
-    return lax.all_gather(basis_part, "token", axis=0, tiled=True)
+    return gather_around(basis_part, "token", 0)
 
 
 def per_device(tokens, routes, assign, gate_weight, up_weight, sketch):

time: 940 us -> 920 us (0.979)
  waiting for transfers between devices: 243 us -> 193 us
  starting transfers between devices: 28 us -> 44.9 us
    all_gather x2 -> x0, waiting for transfers between devices: 69.8 us -> none  [new_basis(): return lax.all_gather(basis_part, 'token', axis=0, tiled=True)]
    ppermute x0 -> x6, waiting for transfers between devices: none -> 21.1 us  [the longest x4 21 us: gather_around(): from_left = lax.ppermute(from_left, axis, forward)]
    ppermute x0 -> x6, starting transfers between devices: none -> 16.9 us  [the longest x2 8.62 us: gather_around(): from_right = lax.ppermute(from_right, axis, backward)]
  transfers between devices with their start and end apart: 9 -> 13, of which waited for: 8 -> 9; matrix products, arithmetic and copies ran while one was open for 18% -> 19% of each run, Pallas kernels for 0% -> 0%
where the time goes in v1:
time: 920 us; the launch traced here: 908 us
  blocking collectives  284 us (31%)
  other arithmetic  244 us (27%)
  waiting for transfers between devices  193 us (21%)
  local copies, waits for them, and re-layouts  67 us (7%)
  matrix products  55.7 us (6%)
  starting transfers between devices  44.9 us (5%)
  between operations  19.5 us (2%)
    all_to_all x2, blocking collectives, new_basis(): lax.all_to_all(pieces, 'expert', split_axis=1, concat_axis=1, tiled=True)  235 us
    another operation x29, other arithmetic, new_basis(): lower_factor = jnp.linalg.cholesky(column_gram)  158 us
    another operation x5, other arithmetic, new_basis(): jax.scipy.linalg.solve_triangular(lower_factor, cluster_rows.astype(jnp.f...  80.9 us
    psum x2, waiting for transfers between devices, new_basis(): lax.psum(local_gram.astype(jnp.bfloat16), 'token').astype(jnp.float32)  51.2 us
    all_to_all x1, waiting for transfers between devices, per_device(): lax.all_to_all(outgoing, 'expert', split_axis=0, concat_axis=0, tiled=True)  50.2 us
    all_to_all x1, blocking collectives, new_basis(): lax.all_to_all(outgoing, 'expert', split_axis=0, concat_axis=0, tiled=True)  48.9 us
    reduce_scatter x2, waiting for transfers between devices, new_basis(): lax.psum_scatter(by_cluster.astype(jnp.bfloat16), 'token', scatter_dimens...  42.2 us
    all_to_all x1, waiting for transfers between devices, new_basis(): lax.all_to_all(outgoing, 'expert', split_axis=0, concat_axis=0, tiled=True)  28 us
  transfers between devices with their start and end apart: 13, of which 9 were waited for; matrix products, arithmetic and copies ran while one was open for 19% of the time, Pallas kernels for 0%

profile of v1, /device:TPU:1, one launch (start us, length us, event | category | flops | bytes accessed | tf_op | source)
XLA Modules:
  0.0 907.8 jit_solution(14689972462395443872)
XLA Ops:
  7.9 2.2 convolution_convert_fusion.1
  11.8 117.2 %all_to_all.25 = bf16[4,512,512]{2,0,1:T(4,128)(2,1)S(1)} all-to-all(bf16[4,512,512]{2,0,1:T(4,128)(2,1)S(1)} %copy.53), channel_id=1, replica_groups=mesh['expert'=128,'token'=4] {'expert'}, dimensions={1} | all-to-all | bytes 4194304 | tf_op jit(solution)/shard_map/all_to_all | solution.py:52
  129.1 3.2 fusion.16
  132.4 22.3 %reduce-scatter.3.cloned.1.call-done = bf16[32,1,4,512]{3,0,2,1:T(8,128)(2,1)} async-done(((bf16[32,4,4,512]{3,0,2,1:T(8,128)(2,1)}), bf16[32,1,4,512]{3,0,2,1:T(8,128)(2,1)}) %reduce-scatter.3.cloned.1.call-update) | async-done | bytes 131088 | tf_op jit(solution)/shard_map/reduce_scatter | solution.py:55
  157.0 48.9 %all_to_all.26 = bf16[128,4,512]{2,1,0:T(4,128)(2,1)S(1)} all-to-all(bf16[128,4,512]{2,1,0:T(4,128)(2,1)S(1)} %select_convert_fusion.1), channel_id=1, replica_groups=mesh['expert'=128,'token'=4] {'expert'}, dimensions={0} | all-to-all | bytes 1048576 | tf_op jit(solution)/shard_map/all_to_all | solution.py:59
  208.9 47.0 %all-reduce.4.cloned.1.call-done = bf16[512,512]{0,1:T(8,128)(2,1)} async-done(((bf16[512,512]{0,1:T(8,128)(2,1)}), bf16[512,512]{0,1:T(8,128)(2,1)}) %all-reduce.4.cloned.1.call-update) | async-done | bytes 524304 | tf_op jit(solution)/shard_map/psum | solution.py:64
  259.4 11.7 %cholesky.286 = f32[128,128]{1,0:T(8,128)S(1)} custom-call(f32[128,128]{1,0:T(8,128)S(1)} %cholesky.426), custom_call_target="Cholesky" | custom-call | tf_op jit(solution)/shard_map/jit(cholesky)/cholesky | solution.py:65
  271.2 9.8 %custom-call.27 = f32[1,128,128]{1,2,0:T(8,128)S(1)} custom-call(f32[1,128,128]{2,1,0:T(8,128)S(1)} %get-tuple-element.67), custom_call_target="InvertDiagBlocksLowerTriangular" | custom-call | tf_op jit(solution)/shard_map/jit(cholesky)/cholesky | solution.py:65
  283.6 11.7 %cholesky.305 = f32[128,128]{1,0:T(8,128)S(1)} custom-call(f32[128,128]{1,0:T(8,128)S(1)} %cholesky.430), custom_call_target="Cholesky" | custom-call | tf_op jit(solution)/shard_map/jit(cholesky)/cholesky | solution.py:65
  295.4 10.0 %custom-call.28 = f32[1,128,128]{1,2,0:T(8,128)S(1)} custom-call(f32[1,128,128]{2,1,0:T(8,128)S(1)} %get-tuple-element.64), custom_call_target="InvertDiagBlocksLowerTriangular" | custom-call | tf_op jit(solution)/shard_map/jit(cholesky)/cholesky | solution.py:65
  307.0 11.7 %cholesky.326 = f32[128,128]{1,0:T(8,128)S(1)} custom-call(f32[128,128]{1,0:T(8,128)S(1)} %cholesky.435), custom_call_target="Cholesky" | custom-call | tf_op jit(solution)/shard_map/jit(cholesky)/cholesky | solution.py:65
  319.4 9.8 %custom-call.29 = f32[1,128,128]{1,2,0:T(8,128)S(1)} custom-call(f32[1,128,128]{2,1,0:T(8,128)S(1)} %get-tuple-element.61), custom_call_target="InvertDiagBlocksLowerTriangular" | custom-call | tf_op jit(solution)/shard_map/jit(cholesky)/cholesky | solution.py:65
  330.6 11.7 %cholesky.343 = f32[128,128]{1,0:T(8,128)S(1)} custom-call(f32[128,128]{1,0:T(8,128)S(1)} %convolution_subtract_fusion.11), custom_call_target="Cholesky" | custom-call | tf_op jit(solution)/shard_map/jit(cholesky)/cholesky | solution.py:65
  347.8 11.5 %while.4 = (s32[]{:T(128)}, f32[512,512]{1,0:T(8,128)}, s32[4,2]{0,1:T(2,128)S(1)}, f32[4,128,128]{2,1,0:T(8,128)S(1)}, s32[]{:T(128)}) while((s32[]{:T(128)}, f32[512,512]{1,0:T(8,128)}, s32[4,2]{0,1:T(2,128)S(1)}, f32[4,128,128]{2,1,0:T(8,128)S(1)}, s32[]{:T(128)}) %tuple.54), condition=%wide.while_cond, body=%wide.while_body.sunk | while | flops 2 | bytes 131181 | solution.py:66
  348.4 2.3 bitcast_dynamic-update-slice_fusion.4
  351.3 2.3 bitcast_dynamic-update-slice_fusion.4
  354.2 2.3 bitcast_dynamic-update-slice_fusion.4
  359.3 39.3 %custom-call.30 = f32[4,128,128]{1,2,0:T(8,128)S(1)} custom-call(f32[4,128,128]{2,1,0:T(8,128)S(1)} %get-tuple-element.22), custom_call_target="InvertDiagBlocksLowerTriangular" | custom-call | tf_op jit(solution)/shard_map/jit(_solve_triangular)/triangular_solve | solution.py:66
  407.3 2.3 collective-permute-start
  409.6 4.2 collective-permute-start.1
  413.8 7.2 collective-permute-done
  424.8 9.1 %collective-permute-done.2 = bf16[512,512]{0,1:T(8,128)(2,1)} collective-permute-done((bf16[512,512]{0,1:T(8,128)(2,1)S(1)}, bf16[512,512]{0,1:T(8,128)(2,1)}, u32[]{:S(2)}, u32[]{:S(2)}) %collective-permute-start.2) | collective-permute-done | bytes 524320 | tf_op jit(solution)/shard_map/ppermute | solution.py:16
  435.8 5.2 fusion
  441.0 4.5 reshape.84
  445.5 6.5 copy.61
  452.0 117.9 %all_to_all.27 = bf16[4,512,512]{2,0,1:T(4,128)(2,1)S(1)} all-to-all(bf16[4,512,512]{2,0,1:T(4,128)(2,1)} %copy.61), channel_id=1, replica_groups=mesh['expert'=128,'token'=4] {'expert'}, dimensions={1} | all-to-all | bytes 4194304 | tf_op jit(solution)/shard_map/all_to_all | solution.py:52
  569.9 3.2 fusion.19
  573.2 19.9 %reduce-scatter.5.cloned.1.call-done = bf16[32,1,4,512]{3,0,2,1:T(8,128)(2,1)} async-done(((bf16[32,4,4,512]{3,0,2,1:T(8,128)(2,1)}), bf16[32,1,4,512]{3,0,2,1:T(8,128)(2,1)}) %reduce-scatter.5.cloned.1.call-update) | async-done | bytes 131088 | tf_op jit(solution)/shard_map/reduce_scatter | solution.py:55
  596.2 18.3 %all-to-all-start.4 = ((bf16[128,4,512]{2,1,0:T(4,128)(2,1)}), bf16[128,4,512]{2,1,0:T(4,128)(2,1)S(1)}, u32[]{:S(2)}, u32[]{:S(2)}) async-start(bf16[128,4,512]{2,1,0:T(4,128)(2,1)} %select_convert_fusion), calls=%async_computation.6 | async-start | bytes 1048576 | tf_op jit(solution)/shard_map/all_to_all | solution.py:59
  617.4 28.0 %all-to-all-done.4 = bf16[128,4,512]{2,1,0:T(4,128)(2,1)S(1)} async-done(((bf16[128,4,512]{2,1,0:T(4,128)(2,1)}), bf16[128,4,512]{2,1,0:T(4,128)(2,1)S(1)}, u32[]{:S(2)}, u32[]{:S(2)}) %all-to-all-start.4) | async-done | bytes 524320 | tf_op jit(solution)/shard_map/all_to_all | solution.py:59
  645.4 9.1 %all-to-all-start = ((bf16[128,2,2048]{2,1,0:T(2,128)(2,1)}), bf16[128,2,2048]{2,1,0:T(2,128)(2,1)S(1)}, u32[]{:S(2)}, u32[]{:S(2)}) async-start(bf16[128,2,2048]{2,1,0:T(2,128)(2,1)} %reshape.80), calls=%async_computation | async-start | bytes 2097152 | tf_op jit(solution)/shard_map/all_to_all | solution.py:96
  656.1 50.2 %all-to-all-done = bf16[128,2,2048]{2,1,0:T(2,128)(2,1)S(1)} async-done(((bf16[128,2,2048]{2,1,0:T(2,128)(2,1)}), bf16[128,2,2048]{2,1,0:T(2,128)(2,1)S(1)}, u32[]{:S(2)}, u32[]{:S(2)}) %all-to-all-start) | async-done | bytes 1048608 | tf_op jit(solution)/shard_map/all_to_all | solution.py:96
  708.8 4.2 all-reduce.6.cloned.1.call-done
  716.5 11.7 %cholesky.358 = f32[128,128]{1,0:T(8,128)S(1)} custom-call(f32[128,128]{1,0:T(8,128)S(1)} %cholesky.439), custom_call_target="Cholesky" | custom-call | tf_op jit(solution)/shard_map/jit(cholesky)/cholesky | solution.py:65
  728.4 9.8 %custom-call.31 = f32[1,128,128]{1,2,0:T(8,128)S(1)} custom-call(f32[1,128,128]{2,1,0:T(8,128)S(1)} %get-tuple-element.57), custom_call_target="InvertDiagBlocksLowerTriangular" | custom-call | tf_op jit(solution)/shard_map/jit(cholesky)/cholesky | solution.py:65
  740.7 11.7 %cholesky.377 = f32[128,128]{1,0:T(8,128)S(1)} custom-call(f32[128,128]{1,0:T(8,128)S(1)} %cholesky.443), custom_call_target="Cholesky" | custom-call | tf_op jit(solution)/shard_map/jit(cholesky)/cholesky | solution.py:65
  752.4 10.2 %custom-call.32 = f32[1,128,128]{1,2,0:T(8,128)S(1)} custom-call(f32[1,128,128]{2,1,0:T(8,128)S(1)} %get-tuple-element.54), custom_call_target="InvertDiagBlocksLowerTriangular" | custom-call | tf_op jit(solution)/shard_map/jit(cholesky)/cholesky | solution.py:65
  764.2 11.7 %cholesky.398 = f32[128,128]{1,0:T(8,128)S(1)} custom-call(f32[128,128]{1,0:T(8,128)S(1)} %cholesky.448), custom_call_target="Cholesky" | custom-call | tf_op jit(solution)/shard_map/jit(cholesky)/cholesky | solution.py:65
  776.0 9.8 %custom-call.33 = f32[1,128,128]{1,2,0:T(8,128)S(1)} custom-call(f32[1,128,128]{2,1,0:T(8,128)S(1)} %get-tuple-element.51), custom_call_target="InvertDiagBlocksLowerTriangular" | custom-call | tf_op jit(solution)/shard_map/jit(cholesky)/cholesky | solution.py:65
  787.2 11.7 %cholesky.415 = f32[128,128]{1,0:T(8,128)S(1)} custom-call(f32[128,128]{1,0:T(8,128)S(1)} %convolution_subtract_fusion.10), custom_call_target="Cholesky" | custom-call | tf_op jit(solution)/shard_map/jit(cholesky)/cholesky | solution.py:65
  805.4 11.3 %while.5 = (s32[]{:T(128)}, f32[512,512]{1,0:T(8,128)}, s32[4,2]{0,1:T(2,128)S(1)}, f32[4,128,128]{2,1,0:T(8,128)S(1)}, s32[]{:T(128)}) while((s32[]{:T(128)}, f32[512,512]{1,0:T(8,128)}, s32[4,2]{0,1:T(2,128)S(1)}, f32[4,128,128]{2,1,0:T(8,128)S(1)}, s32[]{:T(128)}) %tuple.70), condition=%wide.while_cond.clone, body=%wide.while_body.clone.sunk | while | flops 2 | bytes 131181 | solution.py:66
  811.7 2.2 bitcast_dynamic-update-slice_fusion.5
  816.7 39.3 %custom-call.34 = f32[4,128,128]{1,2,0:T(8,128)S(1)} custom-call(f32[4,128,128]{2,1,0:T(8,128)S(1)} %get-tuple-element.23), custom_call_target="InvertDiagBlocksLowerTriangular" | custom-call | tf_op jit(solution)/shard_map/jit(_solve_triangular)/triangular_solve | solution.py:66
  866.8 7.2 reshape.81
  874.1 4.5 collective-permute-start.4
  880.5 6.1 fusion.11
  886.8 4.7 collective-permute-done.5
  894.3 6.7 fusion.13
  (161 shorter events, 87.3 us)
Async XLA Ops:
  6.5 1.4 copy-start
  6.5 148.1 %reduce-scatter.3.cloned.1.call-start = ((), (), s32[]{:S(2)}) async-start(), calls=%async_computation.8 | async-start | bytes 655360 | tf_op jit(solution)/shard_map/reduce_scatter | solution.py:55
  11.8 117.2 %copy-start.12 = (s32[128]{0:T(128)S(1)}, s32[128]{0:T(128)}, u32[]{:S(2)}) copy-start(s32[128]{0:T(128)} %param.13) | copy-start | bytes 1540
  132.3 123.6 %all-reduce.4.cloned.1.call-start = ((), (), s32[]{:S(2)}) async-start(), calls=%async_computation.9 | async-start | bytes 1048576 | tf_op jit(solution)/shard_map/psum | solution.py:64
  207.3 385.8 %reduce-scatter.5.cloned.1.call-start = ((), (), s32[]{:S(2)}) async-start(), calls=%async_computation.10 | async-start | bytes 655360 | tf_op jit(solution)/shard_map/reduce_scatter | solution.py:55
  258.4 1.0 copy-start.4
  347.8 54.0 %copy-start.2 = (f32[512,512]{0,1:T(8,128)S(1)}, f32[512,512]{0,1:T(8,128)}, u32[]{:S(2)}) copy-start(f32[512,512]{0,1:T(8,128)} %copy.60) | copy-start | bytes 3145732
  405.9 1.4 copy-start.9
  407.3 13.7 %collective-permute-start = (bf16[512,512]{0,1:T(8,128)(2,1)S(1)}, bf16[512,512]{0,1:T(8,128)(2,1)S(1)}, u32[]{:S(2)}, u32[]{:S(2)}) collective-permute-start(bf16[512,512]{0,1:T(8,128)(2,1)S(1)} %get-tuple-element.43), channel_id=1, source_target_pairs={{0,1},{1,2},{2,3},{3,0},{4,5},{5,6},{6,7},{7,4},{8,9},{9,10},{10,1... | collective-permute-start | bytes 1572872 | tf_op jit(solution)/shard_map/ppermute | solution.py:16
  409.6 14.2 %collective-permute-start.1 = (bf16[512,512]{0,1:T(8,128)(2,1)S(1)}, bf16[512,512]{0,1:T(8,128)(2,1)S(1)}, u32[]{:S(2)}, u32[]{:S(2)}) collective-permute-start(bf16[512,512]{0,1:T(8,128)(2,1)S(1)} %get-tuple-element.43), channel_id=1, source_target_pairs={{0,3},{1,0},{2,1},{3,2},{4,7},{5,4},{6,5},{7,6},{8,11},{9,8},{10,9... | collective-permute-start | bytes 1572872 | tf_op jit(solution)/shard_map/ppermute | solution.py:21
  421.0 12.9 %collective-permute-start.2 = (bf16[512,512]{0,1:T(8,128)(2,1)S(1)}, bf16[512,512]{0,1:T(8,128)(2,1)}, u32[]{:S(2)}, u32[]{:S(2)}) collective-permute-start(bf16[512,512]{0,1:T(8,128)(2,1)S(1)} %collective-permute-done), channel_id=1, source_target_pairs={{0,1},{1,2},{2,3},{3,0},{4,5},{5,6},{6,7},{7,4},{8,9},{9,10},{10,1... | collective-permute-start | bytes 1572872 | tf_op jit(solution)/shard_map/ppermute | solution.py:16
  573.1 41.4 %copy-start.11 = (s32[16,8]{0,1:T(8,128)S(1)}, s32[16,8]{0,1:T(8,128)}, u32[]{:S(2)}) copy-start(s32[16,8]{0,1:T(8,128)} %param.12) | copy-start | bytes 1540
  573.1 42.3 %copy-start.10 = (bf16[16,2048]{1,0:T(8,128)(2,1)S(1)}, bf16[16,2048]{1,0:T(8,128)(2,1)}, u32[]{:S(2)}) copy-start(bf16[16,2048]{1,0:T(8,128)(2,1)} %param.11) | copy-start | bytes 196612
  596.2 49.1 %all-to-all-start.4 = ((bf16[128,4,512]{2,1,0:T(4,128)(2,1)}), bf16[128,4,512]{2,1,0:T(4,128)(2,1)S(1)}, u32[]{:S(2)}, u32[]{:S(2)}) async-start(bf16[128,4,512]{2,1,0:T(4,128)(2,1)} %select_convert_fusion), calls=%async_computation.6 | async-start | bytes 1048576 | tf_op jit(solution)/shard_map/all_to_all | solution.py:59
  645.4 61.0 %all-to-all-start = ((bf16[128,2,2048]{2,1,0:T(2,128)(2,1)}), bf16[128,2,2048]{2,1,0:T(2,128)(2,1)S(1)}, u32[]{:S(2)}, u32[]{:S(2)}) async-start(bf16[128,2,2048]{2,1,0:T(2,128)(2,1)} %reshape.80), calls=%async_computation | async-start | bytes 2097152 | tf_op jit(solution)/shard_map/all_to_all | solution.py:96
  654.5 58.5 %all-reduce.6.cloned.1.call-start = ((), (), s32[]{:S(2)}) async-start(), calls=%async_computation.11 | async-start | bytes 1048576 | tf_op jit(solution)/shard_map/psum | solution.py:64
  655.8 211.0 %all-gather.2.cloned.1.call-start = ((), (), s32[]{:S(2)}) async-start(), calls=%async_computation.7 | async-start | bytes 5242880 | tf_op jit(solution)/shard_map/all_gather | solution.py:97
  706.3 1.0 copy-start.1
  715.5 1.0 copy-start.5
  805.3 53.8 %copy-start.3 = (f32[512,512]{0,1:T(8,128)S(1)}, f32[512,512]{0,1:T(8,128)}, u32[]{:S(2)}) copy-start(f32[512,512]{0,1:T(8,128)} %copy.68) | copy-start | bytes 3145732
  863.3 1.4 copy-start.6
  864.7 13.9 %collective-permute-start.3 = (bf16[512,512]{0,1:T(8,128)(2,1)S(1)}, bf16[512,512]{0,1:T(8,128)(2,1)S(1)}, u32[]{:S(2)}, u32[]{:S(2)}) collective-permute-start(bf16[512,512]{0,1:T(8,128)(2,1)S(1)} %get-tuple-element.41), channel_id=1, source_target_pairs={{0,1},{1,2},{2,3},{3,0},{4,5},{5,6},{6,7},{7,4},{8,9},{9,10},{10,1... | collective-permute-start | bytes 1572872 | tf_op jit(solution)/shard_map/ppermute | solution.py:16
  874.1 12.6 %copy-start.7 = (bf16[2048,512]{0,1:T(8,128)(2,1)S(1)}, bf16[2048,512]{0,1:T(8,128)(2,1)}, u32[]{:S(2)}) copy-start(bf16[2048,512]{0,1:T(8,128)(2,1)} %copy-done.6) | copy-start | bytes 6291460
  874.1 12.7 %collective-permute-start.4 = (bf16[512,512]{0,1:T(8,128)(2,1)S(1)}, bf16[512,512]{0,1:T(8,128)(2,1)S(1)}, u32[]{:S(2)}, u32[]{:S(2)}) collective-permute-start(bf16[512,512]{0,1:T(8,128)(2,1)S(1)} %get-tuple-element.41), channel_id=1, source_target_pairs={{0,3},{1,0},{2,1},{3,2},{4,7},{5,4},{6,5},{7,6},{8,11},{9,8},{10,9... | collective-permute-start | bytes 1572872 | tf_op jit(solution)/shard_map/ppermute | solution.py:21
  878.5 13.0 %collective-permute-start.5 = (bf16[512,512]{0,1:T(8,128)(2,1)S(1)}, bf16[512,512]{0,1:T(8,128)(2,1)S(1)}, u32[]{:S(2)}, u32[]{:S(2)}) collective-permute-start(bf16[512,512]{0,1:T(8,128)(2,1)S(1)} %collective-permute-done.3), channel_id=1, source_target_pairs={{0,1},{1,2},{2,3},{3,0},{4,5},{5,6},{6,7},{7,4},{8,9},{9,10},{10,1... | collective-permute-start | bytes 1572872 | tf_op jit(solution)/shard_map/ppermute | solution.py:16
  891.6 1.4 copy-start.8
  892.9 1.4 copy-start.13
Sparse Core Ops, SparseCore 0:
  132.4 22.2 reduce-scatter.2
  207.4 48.4 all-reduce.3
  573.3 19.7 reduce-scatter.4
  657.3 55.6 all-reduce.5
  714.9 59.0 all-gather.1
